TPU v7x, 32 devices: a whole 2x2x4 slice. The times are simulated.
32 devices in a mesh: space: 4 (over z), sample: 8 (over y, x, core).
Axes of the slice: x: 2, y: 2, z: 4, core: 2. Of those that a mesh axis runs over, the one named last changes fastest.
Arguments:
- mean_field: float32 [4, 48, 128], P('space'), may hold values from -0.6 to 0.6
- modes: bfloat16 [64, 4, 48, 128], P(None, 'space'), may hold values from -6 to 6
- coeffs: bfloat16 [64, 3072], P(None, 'sample'), may hold values from -6 to 6
- kicks: float32 [64, 3072], P(None, 'sample'), may hold values from -6 to 6
Outputs:
- new_mean: float32 [4, 48, 128], P('space')
- new_modes: float32 [64, 4, 48, 128], P(None, 'space')
- new_coeffs: float32 [64, 3072], P(None, 'sample')
All inputs are finite; a program needn't handle non-finite values.
Results may differ from a plain program's by a relative error of at most 0.0023.
Values may be sent and summed in bfloat16 or wider, within the bound.
A program may use at most 64 MiB of HBM per device.

v0:
```python
import jax
import jax.numpy as jnp
from jax import lax
from jax.sharding import PartitionSpec as P

CELL_BLOCK = 2048


amplitude = 0.1
reaction = 2.0
diffusion = 0.25
time_step = 0.1
noise_level = 0.3


def padded_2(value, sides, width):
    for axis, dim in sides:
        devices, length = (lax.axis_size(axis), value.shape[dim])
        up = [(i, (i + 1) % devices) for i in range(devices - 1)]
        down = [(j, i) for i, j in up]
        last = lax.slice_in_dim(value, length - width, length, axis=dim)
        first = lax.slice_in_dim(value, 0, width, axis=dim)
        before = lax.ppermute(last, axis, up)
        after = lax.ppermute(first, axis, down)
        value = jnp.concatenate([before, value, after], axis=dim)
    return value


def laplace_ext(extended):
    centre = extended[..., 1:-1, :, :]
    pads = [(0, 0)] * (centre.ndim - 2) + [(1, 1), (1, 1)]
    padded = jnp.pad(centre, pads)
    neighbours = extended[..., 2:, :, :] + extended[..., :-2, :, :]
    neighbours = neighbours + padded[..., 2:, 1:-1] + padded[..., :-2, 1:-1]
    neighbours = neighbours + padded[..., 1:-1, 2:] + padded[..., 1:-1, :-2]
    return neighbours - 6.0 * centre


def tile_terms(flat_modes, flat_mean, coeffs, block_len):
    rank_size, cell_count = flat_modes.shape
    local_samples = coeffs.shape[1]
    block_count = cell_count // block_len

    def advance(position, totals):
        mode_acc, coef_acc, react_acc = totals
        offset = position * block_len
        block_modes = lax.dynamic_slice_in_dim(flat_modes, offset, block_len, 1)
        block_mean = lax.dynamic_slice_in_dim(flat_mean, offset, block_len, 0)
        rebuilt = lax.dot_general(
            coeffs, block_modes, (((0,), (0,)), ((), ())), preferred_element_type=jnp.float32
        )
        total_field = block_mean[None, :] + amplitude * rebuilt
        react = (reaction * (total_field - total_field * total_field * total_field)).astype(
            jnp.bfloat16
        )
        mode_blk = jnp.dot(coeffs, react, preferred_element_type=jnp.float32)
        mode_acc = lax.dynamic_update_slice_in_dim(mode_acc, mode_blk, offset, 1)
        coef_acc = coef_acc + lax.dot_general(
            block_modes, react, (((1,), (1,)), ((), ())), preferred_element_type=jnp.float32
        )
        react_acc = lax.dynamic_update_slice_in_dim(
            react_acc, jnp.sum(react.astype(jnp.float32), axis=0), offset, 0
        )
        return (mode_acc, coef_acc, react_acc)

    start_vals = (
        jnp.zeros((rank_size, cell_count), jnp.float32),
        jnp.zeros((rank_size, local_samples), jnp.float32),
        jnp.zeros((cell_count,), jnp.float32),
    )
    return lax.fori_loop(0, block_count, advance, start_vals)


def per_device(mean_field, modes, coeffs, kicks):
    high = lax.Precision.HIGHEST
    rank_size = modes.shape[0]
    planes, rows_y, rows_z = (modes.shape[1], modes.shape[2], modes.shape[3])
    cell_count = planes * rows_y * rows_z
    local_samples = coeffs.shape[1]
    n_sample = lax.axis_size("sample")
    total_cells = cell_count * lax.axis_size("space")
    total_samples = local_samples * n_sample
    mode_ext = padded_2(modes, (("space", 1),), 1)
    mean_ext = padded_2(mean_field, (("space", 0),), 1)
    lap_modes = laplace_ext(mode_ext.astype(jnp.float32)).reshape(rank_size, cell_count)
    lap_mean = laplace_ext(mean_ext).reshape(cell_count)
    flat_modes = modes.reshape(rank_size, cell_count)
    flat_mean = mean_field.reshape(cell_count)
    modes_f = flat_modes.astype(jnp.float32)
    coeff_f = coeffs.astype(jnp.float32)
    stiff_part = (
        lax.dot_general(modes_f, lap_modes, (((1,), (1,)), ((), ())), precision=high) / total_cells
    )
    gram_part = lax.dot_general(
        coeffs, coeffs, (((1,), (1,)), ((), ())), preferred_element_type=jnp.float32
    )
    mode_part, coef_part, react_part = tile_terms(
        flat_modes, flat_mean, coeffs, min(CELL_BLOCK, cell_count)
    )
    mode_force, react_sum, gram_sum = lax.psum((mode_part, react_part, gram_part), "sample")
    coef_force, stiff = lax.psum((coef_part, stiff_part), "space")
    react_mean = react_sum / total_samples
    covariance = gram_sum / total_samples
    chol = jnp.linalg.cholesky(covariance)
    drive = (
        jax.scipy.linalg.cho_solve((chol, True), mode_force / (amplitude * total_samples))
        + diffusion * lap_modes
    )
    correlation_part = lax.dot_general(modes_f, drive, (((1,), (1,)), ((), ())), precision=high)
    shift_part = jnp.dot(modes_f, react_mean, precision=high)
    correlation_sum, shift = lax.psum((correlation_part, shift_part), "space")
    correlation = correlation_sum / total_cells
    moved = drive - jnp.dot(correlation.T, modes_f, precision=high)
    mode_share = modes_f + time_step * moved
    mean_share = flat_mean + time_step * (diffusion * lap_mean + react_mean)
    new_mean = mean_share.reshape(planes, rows_y, rows_z)
    new_modes = mode_share.reshape(rank_size, planes, rows_y, rows_z)
    rate = (coef_force - shift[:, None]) / (amplitude * total_cells) + diffusion * jnp.dot(
        stiff, coeff_f, precision=high
    )
    new_coeffs = coeff_f + time_step * rate + noise_level * time_step**0.5 * kicks
    return (new_mean, new_modes, new_coeffs)


def solution(mesh):
    return jax.shard_map(
        per_device,
        mesh=mesh,
        in_specs=(
            P("space", None, None),
            P(None, "space", None, None),
            P(None, "sample"),
            P(None, "sample"),
        ),
        out_specs=(P("space", None, None), P(None, "space", None, None), P(None, "sample")),
        check_vma=False,
    )
```

profile of v0, /device:TPU:0, one launch (start us, length us, event | category | flops | bytes accessed | tf_op | source)
XLA Modules:
  0.0 131.6 jit_solution(18019876186060634327)
XLA Ops:
  7.2 2.2 %copy.34 = bf16[8,8,48,128]{3,1,2,0:T(8,128)(2,1)} copy(bf16[8,8,48,128]{3,2,1,0:T(8,128)(2,1)} %bitcast.89) | data formatting | bytes 1572864
  9.6 13.0 %while.18 = (s32[]{:T(128)}, f32[64,6144]{1,0:T(8,128)S(1)}, f32[64,384]{1,0:T(8,128)S(1)}, f32[6144]{0:T(1024)S(1)}, f32[6144]{0:T(1024)S(1)}, /*index=5*/bf16[...) while((s32[]{:T(128)}, f32[64,6144]{1,0:T(8,128)S(1)}, ...), condition=%wide.region_2.3_spmd.clone, body=%wide.region_0.2_spmd.clone.sunk | while | flops 309114880 | bytes 6111417 | solution.py:71
  9.6 2.0 %convert_reduce_fusion.2 = (f32[2048]{0:T(1024)S(1)}, bf16[384,2048]{1,0:T(8,128)(2,1)S(1)}) fusion(bf16[64,384]{1,0:T(8,128)(2,1)S(1)} %get-tuple-element.259, bf16[64,6144]{1,0:T(8,128)(2,1)} %get-tuple-element.258, s32[]{:T(128)S(6)} %select_n.20, f32[2048]{0:T(1024)S(1)} %dynamic_slice.27), kind=kOutput, calls=%fused_computation.3.clone.1 | convolution fusion | flops 107739136 | bytes 1900548 | tf_op jit(solution)/shard_map/while/body/eval_jaxpr/dot_general | solution.py:49
  12.1 1.6 %convolution_add_fusion.3 = f32[64,384]{1,0:T(8,128)S(1)} fusion(bf16[384,2048]{1,0:T(8,128)(2,1)S(1)} %get-tuple-element.229, bf16[64,6144]{1,0:T(8,128)(2,1)} %get-tuple-element.258, s32[]{:T(128)S(6)} %select_n.20, f32[64,384]{1,0:T(8,128)S(1)} %get-tuple-element.244, pred[]{:T(512)S(6)} %compare.19), kind=kOutput, calls=%fused_computation.6.clone.1 | convolution fusion | flops 100712448 | bytes 2031621 | tf_op jit(solution)/shard_map/while/body/eval_jaxpr/dot_general | solution.py:58
  14.0 2.0 %convert_reduce_fusion.2 = (f32[2048]{0:T(1024)S(1)}, bf16[384,2048]{1,0:T(8,128)(2,1)S(1)}) fusion(bf16[64,384]{1,0:T(8,128)(2,1)S(1)} %get-tuple-element.259, bf16[64,6144]{1,0:T(8,128)(2,1)} %get-tuple-element.258, s32[]{:T(128)S(6)} %select_n.20, f32[2048]{0:T(1024)S(1)} %dynamic_slice.27), kind=kOutput, calls=%fused_computation.3.clone.1 | convolution fusion | flops 107739136 | bytes 1900548 | tf_op jit(solution)/shard_map/while/body/eval_jaxpr/dot_general | solution.py:49
  16.4 1.6 %convolution_add_fusion.3 = f32[64,384]{1,0:T(8,128)S(1)} fusion(bf16[384,2048]{1,0:T(8,128)(2,1)S(1)} %get-tuple-element.229, bf16[64,6144]{1,0:T(8,128)(2,1)} %get-tuple-element.258, s32[]{:T(128)S(6)} %select_n.20, f32[64,384]{1,0:T(8,128)S(1)} %get-tuple-element.244, pred[]{:T(512)S(6)} %compare.19), kind=kOutput, calls=%fused_computation.6.clone.1 | convolution fusion | flops 100712448 | bytes 2031621 | tf_op jit(solution)/shard_map/while/body/eval_jaxpr/dot_general | solution.py:58
  18.4 2.0 %convert_reduce_fusion.2 = (f32[2048]{0:T(1024)S(1)}, bf16[384,2048]{1,0:T(8,128)(2,1)S(1)}) fusion(bf16[64,384]{1,0:T(8,128)(2,1)S(1)} %get-tuple-element.259, bf16[64,6144]{1,0:T(8,128)(2,1)} %get-tuple-element.258, s32[]{:T(128)S(6)} %select_n.20, f32[2048]{0:T(1024)S(1)} %dynamic_slice.27), kind=kOutput, calls=%fused_computation.3.clone.1 | convolution fusion | flops 107739136 | bytes 1900548 | tf_op jit(solution)/shard_map/while/body/eval_jaxpr/dot_general | solution.py:49
  20.8 1.6 %convolution_add_fusion.3 = f32[64,384]{1,0:T(8,128)S(1)} fusion(bf16[384,2048]{1,0:T(8,128)(2,1)S(1)} %get-tuple-element.229, bf16[64,6144]{1,0:T(8,128)(2,1)} %get-tuple-element.258, s32[]{:T(128)S(6)} %select_n.20, f32[64,384]{1,0:T(8,128)S(1)} %get-tuple-element.244, pred[]{:T(512)S(6)} %compare.19), kind=kOutput, calls=%fused_computation.6.clone.1 | convolution fusion | flops 100712448 | bytes 2031621 | tf_op jit(solution)/shard_map/while/body/eval_jaxpr/dot_general | solution.py:58
  22.7 1.1 copy-done.1
  23.9 0.5 copy-done
  24.4 5.0 %collective-permute-start.2 = (bf16[64,1,48,128]{3,2,1,0:T(8,128)(2,1)S(1)}, bf16[64,1,48,128]{3,2,1,0:T(8,128)(2,1)S(1)}, u32[]{:S(2)}, u32[]{:S(2)}) collective-permute-start(bf16[64,1,48,128]{3,2,1,0:T(8,128)(2,1)S(1)} %copy-done), channel_id=1, source_target_pairs={{0,8},{8,16},{16,24},{1,9},{9,17},{17,25},{2,10},{10,18},{18,26},{... | collective-permute-start | bytes 2359304 | tf_op jit(solution)/shard_map/ppermute | solution.py:23
  29.3 1.3 collective-permute-start.3
  30.6 1.3 collective-permute-start
  31.9 5.2 %collective-permute-start.1 = (f32[1,48,128]{2,1,0:T(8,128)S(1)}, f32[1,48,128]{2,1,0:T(8,128)S(1)}, u32[]{:S(2)}, u32[]{:S(2)}) collective-permute-start(f32[1,48,128]{2,1,0:T(8,128)S(1)} %bitcast.100), channel_id=1, source_target_pairs={{0,8},{8,16},{16,24},{1,9},{9,17},{17,25},{2,10},{10,18},{18,26},{... | collective-permute-start | bytes 73736 | tf_op jit(solution)/shard_map/ppermute | solution.py:23
  37.3 23.8 %all-reduce.2 = (f32[6144]{0:T(1024)S(1)}, f32[64,64]{0,1:T(8,128)S(1)}) all-reduce(f32[6144]{0:T(1024)S(1)} %get-tuple-element.129, f32[64,64]{0,1:T(8,128)S(1)} %fusion.54), channel_id=1, replica_groups=mesh['space'=4,'sample'=8] {'sample'}, use_global_device_ids=true, to_apply=%region_3.4 | all-reduce | flops 10240 | bytes 81920 | tf_op jit(solution)/shard_map/psum | solution.py:100
  61.2 5.8 %cholesky.16 = f32[64,64]{1,0:T(8,128)S(1)} custom-call(f32[64,64]{1,0:T(8,128)S(1)} %fusion.37), custom_call_target="Cholesky" | custom-call | tf_op jit(solution)/shard_map/jit(cholesky)/cholesky | solution.py:104
  67.1 0.6 compare_reduce_fusion
  67.7 0.7 fusion.34
  68.4 4.9 %custom-call.10 = f32[1,64,64]{1,2,0:T(8,128)S(1)} custom-call(f32[1,64,64]{2,1,0:T(8,128)S(1)} %fusion.34), custom_call_target="InvertDiagBlocksLowerTriangular" | custom-call | tf_op jit(solution)/shard_map/jit(_cho_solve)/triangular_solve | solution.py:106
  73.3 0.7 broadcast_multiply_fusion.2
  74.0 0.7 convolution_bitcast_fusion.2
  75.2 2.5 %broadcast_multiply_fusion = (f32[64,1,48,128]{3,2,1,0:T(8,128)}, f32[64,1,48,128]{3,2,1,0:T(8,128)}) fusion(f32[64,1,48,128]{3,2,1,0:T(8,128)S(1)} %slice.64, f32[64,3,48,128]{3,2,1,0:T(8,128)S(1)} %maximum_convert_fusion), kind=kLoop, calls=%fused_computation.43 | loop fusion | flops 3145728 | bytes 7864320 | tf_op jit(solution)/shard_map/mul | solution.py:107
  77.7 8.7 %all-reduce.7.cloned.1.call-done = f32[64,6144]{1,0:T(8,128)} async-done(((f32[64,6144]{1,0:T(8,128)}), f32[64,6144]{1,0:T(8,128)}) %all-reduce.7.cloned.1.call-update) | async-done | bytes 1572880 | tf_op jit(solution)/shard_map/psum | solution.py:100
  86.4 3.0 %fusion.16 = f32[64,6144]{1,0:T(8,128)S(1)} fusion(f32[64,6144]{1,0:T(8,128)} %all-reduce.7.cloned.1.call-done, f32[1,64,64]{1,2,0:T(8,128)S(1)} %custom-call.10), kind=kOutput, calls=%fused_computation.28 | convolution fusion | flops 302383104 | bytes 3162112 | tf_op jit(solution)/shard_map/jit(_cho_solve)/triangular_solve | solution.py:106
  89.4 2.0 %convolution_add_fusion.1 = f32[64,6144]{1,0:T(8,128)S(1)} fusion(f32[64,6144]{1,0:T(8,128)S(1)} %fusion.16, f32[8,8,48,128]{3,2,1,0:T(8,128)S(1)} %bitcast.95, f32[1,64,64]{1,2,0:T(8,128)S(1)} %custom-call.10), kind=kOutput, calls=%fused_computation.12 | convolution fusion | flops 302383104 | bytes 4734976 | tf_op jit(solution)/shard_map/jit(_cho_solve)/triangular_solve | solution.py:106
  91.4 0.9 convolution_bitcast_fusion.1
  92.8 1.4 %fusion.29 = f32[64,64]{1,0:T(8,128)S(1)} fusion(f32[64,48,128]{2,1,0:T(8,128)S(1)} %bitcast.94, bf16[64,48,128]{2,1,0:T(8,128)(2,1)S(1)} %bitcast.92), kind=kOutput, calls=%fused_computation.39 | convolution fusion | flops 301993984 | bytes 2375680 | tf_op jit(solution)/shard_map/dot_general | solution.py:92
  94.2 20.1 %all-reduce.3 = (f32[64,64]{0,1:T(8,128)S(1)}, f32[64,64]{1,0:T(8,128)S(1)}, f32[64]{0:T(128)S(1)}) all-reduce(f32[64,64]{0,1:T(8,128)S(1)} %convolution_bitcast_fusion.1, f32[64,64]{1,0:T(8,128)S(1)} %fusion.29, f32[64]{0:T(128)S(1)} %convolution_bitcast_fusion.2), channel_id=1, replica_groups=mesh['space'=4,'sample'=8] {'space'}, use_global_device_ids=true, to_apply=%region_8.9 | all-reduce | flops 8256 | bytes 66048 | tf_op jit(solution)/shard_map/psum | solution.py:111
  114.3 1.0 fusion.18
  115.3 1.4 %copy.15 = f32[8,8,48,128]{3,2,1,0:T(8,128)} copy(f32[8,8,48,128]{3,1,2,0:T(8,128)S(1)} %fusion.18) | data formatting | bytes 3145728
  116.7 6.3 %all-reduce.9.cloned.1.call-done = f32[64,384]{1,0:T(8,128)} async-done(((f32[64,384]{1,0:T(8,128)}), f32[64,384]{1,0:T(8,128)}) %all-reduce.9.cloned.1.call-update) | async-done | bytes 98320 | tf_op jit(solution)/shard_map/psum | solution.py:101
  123.1 1.7 %fusion.22 = f32[64,384]{1,0:T(8,128)} fusion(f32[64,64]{1,0:T(8,128)S(1)} %get-tuple-element.176, bf16[64,384]{1,0:T(8,128)(2,1)S(1)} %get-tuple-element.272, f32[64,384]{1,0:T(8,128)S(1)} %copy-done.7, f32[64,384]{1,0:T(8,128)} %all-reduce.9.cloned.1.call-done, f32[64]{0:T(128)S(1)} %get-tuple-element.177), kind=kOutput, calls=%fused_computation.35 | convolution fusion | flops 19095552 | bytes 360704 | tf_op jit(solution)/shard_map/dot_general | solution.py:118
  (41 shorter events, 3.6 us)
Async XLA Ops:
  7.2 79.3 %all-reduce.7.cloned.1.call-start = ((), (), s32[]{:S(2)}) async-start(), calls=%async_computation | async-start | bytes 3145728 | tf_op jit(solution)/shard_map/psum | solution.py:100
  7.2 2.4 %copy-start.5 = (bf16[64,384]{1,0:T(8,128)(2,1)S(1)}, bf16[64,384]{1,0:T(8,128)(2,1)}, u32[]{:S(2)}) copy-start(bf16[64,384]{1,0:T(8,128)(2,1)} %param.8) | copy-start | bytes 147460
  7.2 2.4 %copy-start.6 = (f32[1,48,128]{2,1,0:T(8,128)S(1)}, f32[1,48,128]{2,1,0:T(8,128)}, u32[]{:S(2)}) copy-start(f32[1,48,128]{2,1,0:T(8,128)} %param.6) | copy-start | bytes 73732
  22.7 1.1 copy-start.1
  22.7 14.5 %copy-start.4 = (f32[64,384]{1,0:T(8,128)}, f32[64,384]{1,0:T(8,128)S(1)}, u32[]{:S(2)}) copy-start(f32[64,384]{1,0:T(8,128)S(1)} %get-tuple-element.131) | copy-start | bytes 294916
  22.7 1.7 %copy-start = (bf16[64,1,48,128]{3,2,1,0:T(8,128)(2,1)S(1)}, bf16[64,1,48,128]{3,2,1,0:T(8,128)(2,1)}, u32[]{:S(2)}) copy-start(bf16[64,1,48,128]{3,2,1,0:T(8,128)(2,1)} %param.7) | copy-start | bytes 2359300
  23.8 99.2 %all-reduce.9.cloned.1.call-start = ((), (), s32[]{:S(2)}) async-start(), calls=%async_computation.1 | async-start | bytes 196608 | tf_op jit(solution)/shard_map/psum | solution.py:101
  24.4 50.3 %collective-permute-start.2 = (bf16[64,1,48,128]{3,2,1,0:T(8,128)(2,1)S(1)}, bf16[64,1,48,128]{3,2,1,0:T(8,128)(2,1)S(1)}, u32[]{:S(2)}, u32[]{:S(2)}) collective-permute-start(bf16[64,1,48,128]{3,2,1,0:T(8,128)(2,1)S(1)} %copy-done), channel_id=1, source_target_pairs={{0,8},{8,16},{16,24},{1,9},{9,17},{17,25},{2,10},{10,18},{18,26},{... | collective-permute-start | bytes 2359304 | tf_op jit(solution)/shard_map/ppermute | solution.py:23
  29.3 45.4 %collective-permute-start.3 = (bf16[64,1,48,128]{3,2,1,0:T(8,128)(2,1)S(1)}, bf16[64,1,48,128]{3,2,1,0:T(8,128)(2,1)S(1)}, u32[]{:S(2)}, u32[]{:S(2)}) collective-permute-start(bf16[64,1,48,128]{3,2,1,0:T(8,128)(2,1)S(1)} %copy-done), channel_id=1, source_target_pairs={{8,0},{16,8},{24,16},{9,1},{17,9},{25,17},{10,2},{18,10},{26,18},{... | collective-permute-start | bytes 2359304 | tf_op jit(solution)/shard_map/ppermute | solution.py:24
  30.6 42.6 %collective-permute-start = (f32[1,48,128]{2,1,0:T(8,128)S(1)}, f32[1,48,128]{2,1,0:T(8,128)S(1)}, u32[]{:S(2)}, u32[]{:S(2)}) collective-permute-start(f32[1,48,128]{2,1,0:T(8,128)S(1)} %bitcast.99), channel_id=1, source_target_pairs={{8,0},{16,8},{24,16},{9,1},{17,9},{25,17},{10,2},{18,10},{26,18},{... | collective-permute-start | bytes 73736 | tf_op jit(solution)/shard_map/ppermute | solution.py:24
  31.9 41.4 %collective-permute-start.1 = (f32[1,48,128]{2,1,0:T(8,128)S(1)}, f32[1,48,128]{2,1,0:T(8,128)S(1)}, u32[]{:S(2)}, u32[]{:S(2)}) collective-permute-start(f32[1,48,128]{2,1,0:T(8,128)S(1)} %bitcast.100), channel_id=1, source_target_pairs={{0,8},{8,16},{16,24},{1,9},{9,17},{17,25},{2,10},{10,18},{18,26},{... | collective-permute-start | bytes 73736 | tf_op jit(solution)/shard_map/ppermute | solution.py:23
  86.4 3.0 %copy-start.3 = (f32[64,1,48,128]{3,2,1,0:T(8,128)S(1)}, f32[64,1,48,128]{3,2,1,0:T(8,128)}, u32[]{:S(2)}) copy-start(f32[64,1,48,128]{3,2,1,0:T(8,128)} %get-tuple-element.178) | copy-start | bytes 4718596
  91.4 1.4 %copy-start.2 = (f32[64,1,48,128]{3,2,1,0:T(8,128)S(1)}, f32[64,1,48,128]{3,2,1,0:T(8,128)}, u32[]{:S(2)}) copy-start(f32[64,1,48,128]{3,2,1,0:T(8,128)} %get-tuple-element.179) | copy-start | bytes 4718596
  115.3 7.8 %copy-start.7 = (f32[64,384]{1,0:T(8,128)S(1)}, f32[64,384]{1,0:T(8,128)}, u32[]{:S(2)}) copy-start(f32[64,384]{1,0:T(8,128)} %param.9) | copy-start | bytes 294916
Sparse Core Ops, SparseCore 0:
  23.9 62.4 all-reduce.6
  89.4 33.5 all-reduce.8
where the time goes:
time: 132 us
  blocking collectives  43.9 us (33%)
  matrix products  22.7 us (17%)
  other arithmetic  15.6 us (12%)
  waiting for transfers between devices  15.1 us (11%)
  between operations  14.3 us (11%)
  starting transfers between devices  12.8 us (10%)
  local copies, waits for them, and re-layouts  7.04 us (5%)
    psum x1, blocking collectives, per_device(): lax.psum((mode_part, react_part, gram_part), 'sample')  23.8 us
    psum x1, blocking collectives, per_device(): correlation_sum, shift = lax.psum((correlation_part, shift_part), 'space')  20.1 us
    ppermute x2, starting transfers between devices, padded_2(): before = lax.ppermute(last, axis, up)  10.1 us
    psum x1, waiting for transfers between devices, per_device(): lax.psum((mode_part, react_part, gram_part), 'sample')  8.71 us
    another operation x3, other arithmetic, per_device(): chol = jnp.linalg.cholesky(covariance)  6.52 us
    psum x1, waiting for transfers between devices, per_device(): coef_force, stiff = lax.psum((coef_part, stiff_part), 'space')  6.31 us
    dot_general x3, matrix products, advance(): lax.dot_general(coeffs, block_modes, (((0,), (0,)), ((), ())), preferred_...  6.01 us
    unnamed x18, local copies, waits for them, and re-layouts  5.78 us
  transfers between devices with their start and end apart: 6, of which 2 were waited for; matrix products, arithmetic and copies ran while one was open for 20% of the time, Pallas kernels for 0%

commit v1 on v0

v1 whole, which is shorter than its diff:
```python
import functools

import jax
import jax.numpy as jnp
from jax import lax
from jax.experimental import pallas as pl
from jax.experimental.pallas import tpu as pltpu
from jax.sharding import PartitionSpec as P

MESH = pl.DeviceIdType.MESH
F32 = jnp.float32
BF16 = jnp.bfloat16
HIGH = lax.Precision.HIGHEST

amplitude = 0.1
reaction = 2.0
diffusion = 0.25
time_step = 0.1
noise_level = 0.3


def dot_nt(a, b, precision=None):
    return lax.dot_general(
        a, b, (((1,), (1,)), ((), ())), precision=precision, preferred_element_type=F32
    )


def dot_nn(a, b, precision=None):
    return jnp.dot(a, b, precision=precision, preferred_element_type=F32)


def rows_of(parts, shape):
    row = lax.broadcasted_iota(jnp.int32, shape, 0)
    block = jnp.zeros(shape, F32)
    for i, part in enumerate(parts):
        block = jnp.where(row == i, part, block)
    return block


def split(value):
    high = value.astype(BF16).astype(F32)
    return high, value - high


def invert(a):
    n = a.shape[0]
    lane = lax.broadcasted_iota(jnp.int32, (1, a.shape[1]), 1)
    row_id = lax.broadcasted_iota(jnp.int32, (n, 1), 0)
    for k in range(n):
        col = a[:, k : k + 1]
        row = a[k : k + 1, :]
        pivot = 1.0 / row[:, k : k + 1]
        row = jnp.where(lane == k, 1.0, row) * pivot
        a = jnp.where(lane == k, 0.0, a) - col * row
        a = jnp.where(row_id == k, row, a)
    return a


def kernel(
    nz, ns, blk, gz,
    mean_ref, modes_ref, coeffs_ref, kicks_ref,
    mean_out, modes_out, coeffs_out,
    maug, caug, ctaug, before, after, rbuf, gacc, fsend, frecv, gath,
    m1s, m1z, m2s, m2z, gbuf,
    h_ss, h_rs, f_ss, f_rs, u_ss, u_rs, g_ss, g_rs,
    a_ss, a_rs, b_ss, b_rs, c_ss, c_rs, d_ss, d_rs,
):
    z = lax.axis_index("space")
    s = lax.axis_index("sample")
    rank, cells = modes_ref.shape
    samples = coeffs_ref.shape[1]
    aug = maug.shape[0]
    total_cells = cells * nz
    total_samples = samples * ns

    barrier = pltpu.get_barrier_semaphore()
    for k in range(1, ns):
        pl.semaphore_signal(
            barrier, inc=1, device_id={"sample": lax.rem(s + k, ns)}, device_id_type=MESH
        )
    for k in range(1, nz):
        pl.semaphore_signal(
            barrier, inc=1, device_id={"space": lax.rem(z + k, nz)}, device_id_type=MESH
        )

    def peer_copy(src, dst, send, recv, axis, me, n, k):
        return pltpu.make_async_remote_copy(
            src_ref=src,
            dst_ref=dst.at[k],
            send_sem=send.at[k - 1],
            recv_sem=recv.at[k - 1],
            device_id={axis: lax.rem(me + k, n)},
            device_id_type=MESH,
        )

    def send_all(buf, send, recv, axis, me, n):
        for k in range(1, n):
            peer_copy(buf.at[0], buf, send, recv, axis, me, n, k).start()

    def sum_all(buf, send, recv, axis, me, n):
        for k in range(1, n):
            peer_copy(buf.at[0], buf, send, recv, axis, me, n, k).wait_recv()
        total = buf[me].astype(F32)
        for j in range(1, n):
            total = total + buf[lax.rem(me - j + n, n)].astype(F32)
        return total

    def drain(buf, send, recv, axis, me, n):
        for k in range(1, n):
            peer_copy(buf.at[0], buf, send, recv, axis, me, n, k).wait_send()

    maug[:, :gz] = jnp.zeros((aug, gz), BF16)
    maug[:, gz + cells :] = jnp.zeros((aug, gz), BF16)
    maug[:rank, gz : gz + cells] = modes_ref[...]
    mean = mean_ref[...]
    hi, rest = split(mean)
    mid, low = split(rest)
    maug[rank:, gz : gz + cells] = rows_of((hi, mid, low), (aug - rank, cells)).astype(BF16)

    pl.semaphore_wait(barrier, ns + nz - 2)

    own = pl.multiple_of(s * blk, blk)
    halo = maug.at[:, pl.ds(pl.multiple_of(own + gz, gz), blk)]
    to_up = pltpu.make_async_remote_copy(
        src_ref=halo, dst_ref=before, send_sem=h_ss.at[0], recv_sem=h_rs.at[0],
        device_id={"space": lax.rem(z + 1, nz)}, device_id_type=MESH,
    )
    to_down = pltpu.make_async_remote_copy(
        src_ref=halo, dst_ref=after, send_sem=h_ss.at[1], recv_sem=h_rs.at[1],
        device_id={"space": lax.rem(z + nz - 1, nz)}, device_id_type=MESH,
    )

    @pl.when(z < nz - 1)
    def _():
        to_up.start()

    @pl.when(z > 0)
    def _():
        to_down.start()

    coeff_f = coeffs_ref[...].astype(F32)
    pad = jnp.where(
        lax.broadcasted_iota(jnp.int32, (caug.shape[0] - rank, samples), 0) < 3, 10.0, 0.0
    )
    full = jnp.concatenate([coeff_f, pad], axis=0)
    caug[...] = full.astype(BF16)
    ctaug[...] = full.T.astype(BF16)
    gacc[...] = jnp.zeros_like(gacc)

    sub = 256 if blk % 256 == 0 else 128

    def block(k, carry):
        owner = lax.rem(s + k, ns)
        base = pl.multiple_of(owner * blk, blk)
        for j in range(blk // sub):
            at = pl.multiple_of(base + (gz + j * sub), 128)
            u = amplitude * dot_nn(ctaug[:, :aug], maug[:, pl.ds(at, sub)])
            r = (reaction * (u - u * u * u)).astype(BF16)
            rbuf[:, j * sub : (j + 1) * sub] = r
        r = rbuf[...]
        f = dot_nn(caug[:aug, :], r)
        gacc[...] += dot_nt(maug[:rank, pl.ds(pl.multiple_of(base + gz, 128), blk)], r)
        fsend[k] = f[: rank + 8]

        @pl.when(k < ns)
        def _():
            pltpu.make_async_remote_copy(
                src_ref=fsend.at[k], dst_ref=frecv.at[k],
                send_sem=f_ss.at[k - 1], recv_sem=f_rs.at[k - 1],
                device_id={"sample": owner}, device_id_type=MESH,
            ).start()

        return carry

    first = ns // 4
    lax.fori_loop(1, 1 + first, block, 0)

    @pl.when(z > 0)
    def _():
        to_up.wait_recv()

    @pl.when(z == 0)
    def _():
        before[...] = jnp.zeros_like(before)

    @pl.when(z < nz - 1)
    def _():
        to_down.wait_recv()

    @pl.when(z == nz - 1)
    def _():
        after[...] = jnp.zeros_like(after)

    gap = jnp.abs(
        lax.broadcasted_iota(jnp.int32, (gz, gz), 0) - lax.broadcasted_iota(jnp.int32, (gz, gz), 1)
    )
    line = jnp.where(gap == 0, -6.0, jnp.where(gap == 1, 1.0, 0.0)).astype(BF16)

    def laplace():
        parts = []
        for j in range(blk // gz):
            at = own + (gz + j * gz)
            centre = maug[:, pl.ds(pl.multiple_of(at, gz), gz)]
            part = dot_nn(centre, line)
            for d in (-gz, gz):
                part = part + maug[:, pl.ds(pl.multiple_of(at + d, gz), gz)].astype(F32)
            part = part + before[:, j * gz : (j + 1) * gz].astype(F32)
            part = part + after[:, j * gz : (j + 1) * gz].astype(F32)
            parts.append(part)
        return jnp.concatenate(parts, axis=1)

    lap = laplace()
    own_modes = maug[:rank, pl.ds(pl.multiple_of(own + gz, 128), blk)]
    lap_hi, lap_lo = split(lap[:rank])
    zero_blk = jnp.zeros((rank, blk), BF16)
    packed = dot_nt(own_modes, jnp.concatenate([zero_blk, lap_hi.astype(BF16)], axis=0))
    packed += dot_nt(own_modes, jnp.concatenate([zero_blk, lap_lo.astype(BF16)], axis=0))
    coeffs = coeffs_ref[...]
    packed += dot_nt(coeffs, jnp.concatenate([coeffs, jnp.zeros_like(coeffs)], axis=0))
    m1s[0] = packed
    st1 = (m1s, a_ss, a_rs, "sample", s, ns)
    send_all(*st1)

    second = ns // 2
    lax.fori_loop(1 + first, 1 + second, block, 0)
    m1z[0] = sum_all(*st1)
    st2 = (m1z, b_ss, b_rs, "space", z, nz)
    send_all(*st2)
    lax.fori_loop(1 + second, 1 + ns, block, 0)

    g = gacc[...]
    m2s[0] = dot_nt(g, caug[...].astype(F32), HIGH)
    st3 = (m2s, c_ss, c_rs, "sample", s, ns)
    send_all(*st3)
    gbuf[0] = g

    m1_sum = sum_all(*st2)
    cov = jnp.where(
        lax.broadcasted_iota(jnp.int32, (rank, 2 * rank), 1) < rank, m1_sum, 0.0
    ) * (1.0 / (nz * total_samples))
    inverse = invert(cov)
    stiff = pltpu.roll(m1_sum, rank, 1)[:, :rank] * (1.0 / total_cells)

    m2z[0] = sum_all(*st3)
    st4 = (m2z, d_ss, d_rs, "space", z, nz)
    send_all(*st4)
    st5 = (gbuf, g_ss, g_rs, "space", z, nz)
    send_all(*st5)

    force = fsend[ns]
    for k in range(1, ns):
        peer_copy(fsend.at[k], frecv, f_ss, f_rs, "sample", s, ns, k).wait_recv()
        force = force + frecv[k]
    solved = dot_nn(inverse[:, :rank], force[:rank], HIGH) * (1.0 / total_samples)
    partial = solved + (time_step * diffusion) * lap[:rank]
    react_mean = force[rank : rank + 1] * (1.0 / (10.0 * total_samples))
    lap_mean = lap[rank : rank + 1] + lap[rank + 1 : rank + 2] + lap[rank + 2 : rank + 3]
    mean_upd = time_step * (diffusion * lap_mean + react_mean)
    gath[0, rank:, :] = rows_of(split(mean_upd), (aug - rank, blk)).astype(BF16)

    m2_sum = sum_all(*st4)
    weights = dot_nt(inverse, m2_sum, HIGH) * (1.0 / (float(total_samples) * total_cells))
    weights = weights + (time_step * diffusion) * stiff
    update = partial - dot_nn(weights, own_modes.astype(F32), HIGH)
    gath[0, :rank, :] = update.astype(BF16)
    st6 = (gath, u_ss, u_rs, "sample", s, ns)
    send_all(*st6)

    coef_force = sum_all(*st5)
    shift = m2_sum[:, rank : rank + 1] * (1.0 / (10.0 * total_samples))
    coeff_f = coeffs_ref[...].astype(F32)
    rate = (coef_force - shift) * (1.0 / (amplitude * total_cells))
    rate = rate + diffusion * dot_nn(stiff, coeff_f, HIGH)
    coeffs_out[...] = coeff_f + time_step * rate + (noise_level * time_step**0.5) * kicks_ref[...]

    def finish(k):
        base = pl.multiple_of(lax.rem(s - k + ns, ns) * blk, blk)
        cols = pl.ds(base, blk)
        old = maug[:rank, pl.ds(pl.multiple_of(base + gz, 128), blk)].astype(F32)
        modes_out[:, cols] = old + gath[k, :rank, :].astype(F32)
        tail = gath[k, rank:, :].astype(F32)
        mean_out[:, cols] = mean_ref[:, cols] + (tail[0:1] + tail[1:2])

    finish(0)
    for k in range(1, ns):
        peer_copy(gath.at[0], gath, u_ss, u_rs, "sample", s, ns, k).wait_recv()
        finish(k)

    for stage in (st1, st2, st3, st4, st5, st6):
        drain(*stage)
    for k in range(1, ns):
        peer_copy(fsend.at[k], frecv, f_ss, f_rs, "sample", s, ns, k).wait_send()

    @pl.when(z < nz - 1)
    def _():
        to_up.wait_send()

    @pl.when(z > 0)
    def _():
        to_down.wait_send()


def per_device(nz, ns, mean_field, modes, coeffs, kicks):
    rank, planes, gy, gz = modes.shape
    cells = planes * gy * gz
    samples = coeffs.shape[1]
    blk = cells // ns
    aug = rank + 16
    wide = 2 * rank
    dma = pltpu.SemaphoreType.DMA
    vm = pltpu.VMEM
    scratch = [
        vm((aug, cells + 2 * gz), BF16),
        vm((wide, samples), BF16),
        vm((samples, wide), BF16),
        vm((aug, blk), BF16),
        vm((aug, blk), BF16),
        vm((samples, blk), BF16),
        vm((rank, samples), F32),
        vm((ns + 1, rank + 8, blk), F32),
        vm((ns, rank + 8, blk), F32),
        vm((ns, aug, blk), BF16),
        vm((ns, rank, wide), F32),
        vm((nz, rank, wide), F32),
        vm((ns, rank, wide), F32),
        vm((nz, rank, wide), F32),
        vm((nz, rank, samples), F32),
    ]
    scratch += [dma((2,)), dma((2,))]
    for n in (ns, ns, nz, ns, nz, ns, nz):
        scratch += [dma((n - 1,)), dma((n - 1,))]
    spec = pl.BlockSpec(memory_space=pltpu.VMEM)
    out = pl.pallas_call(
        functools.partial(kernel, nz, ns, blk, gz),
        out_shape=(
            jax.ShapeDtypeStruct((1, cells), F32),
            jax.ShapeDtypeStruct((rank, cells), F32),
            jax.ShapeDtypeStruct((rank, samples), F32),
        ),
        in_specs=[spec] * 4,
        out_specs=(spec,) * 3,
        scratch_shapes=scratch,
        compiler_params=pltpu.CompilerParams(
            collective_id=0, has_side_effects=True, vmem_limit_bytes=40 * 2**20
        ),
        name="step",
    )(mean_field.reshape(1, cells), modes.reshape(rank, cells), coeffs, kicks)
    new_mean, new_modes, new_coeffs = out
    return (
        new_mean.reshape(planes, gy, gz),
        new_modes.reshape(rank, planes, gy, gz),
        new_coeffs,
    )


def solution(mesh):
    nz, ns = mesh.shape["space"], mesh.shape["sample"]
    return jax.shard_map(
        functools.partial(per_device, nz, ns),
        mesh=mesh,
        in_specs=(
            P("space", None, None),
            P(None, "space", None, None),
            P(None, "sample"),
            P(None, "sample"),
        ),
        out_specs=(P("space", None, None), P(None, "space", None, None), P(None, "sample")),
        check_vma=False,
    )
```

time: 132 us -> 57.9 us (0.44)
  Pallas kernels: 0 us -> 52.3 us
  blocking collectives: 43.9 us -> 0 us
  matrix products: 22.7 us -> 0 us
  other arithmetic: 15.6 us -> 0 us
  waiting for transfers between devices: 15.1 us -> 0 us
  between operations: 14.3 us -> 0.69 us
  starting transfers between devices: 12.8 us -> 0 us
  local copies, waits for them, and re-layouts: 7.04 us -> 4.06 us
    pallas_call x0 -> x1, Pallas kernels: none -> 52.3 us  [per_device(): pl.pallas_call(functools.partial(kernel, nz, ns, blk, gz), out_shape=(jax...]
    psum x2 -> x0, blocking collectives: 43.9 us -> none  [the longest x1 23.8 us: per_device(): lax.psum((mode_part, react_part, gram_part), 'sample')]
    dot_general x15 -> x0, matrix products: 17.8 us -> none  [the longest x3 6.01 us: advance(): lax.dot_general(coeffs, block_modes, (((0,), (0,)), ((), ())), preferred_...]
    psum x2 -> x0, waiting for transfers between devices: 15 us -> none  [the longest x1 8.71 us: per_device(): lax.psum((mode_part, react_part, gram_part), 'sample')]
    ppermute x4 -> x0, starting transfers between devices: 12.7 us -> none  [the longest x2 10.1 us: padded_2(): before = lax.ppermute(last, axis, up)]
    another operation x5 -> x0, other arithmetic: 12.1 us -> none  [the longest x3 6.52 us: per_device(): chol = jnp.linalg.cholesky(covariance)]
    another operation x2 -> x0, matrix products: 4.97 us -> none  [per_device(): jax.scipy.linalg.cho_solve((chol, True), mode_force / (amplitude * total_...]
    mul x1 -> x0, other arithmetic: 2.54 us -> none  [per_device(): diffusion * lap_modes]
  transfers between devices with their start and end apart: 6 -> 0, of which waited for: 2 -> 0; matrix products, arithmetic and copies ran while one was open for 20% -> 0% of each run, Pallas kernels for 0% -> 0%
where the time goes in v1:
time: 57.9 us; the launch traced here: 57.1 us
  Pallas kernels  52.3 us (90%)
  local copies, waits for them, and re-layouts  4.06 us (7%)
  between operations  0.69 us (1%)
    pallas_call x1, Pallas kernels, per_device(): pl.pallas_call(functools.partial(kernel, nz, ns, blk, gz), out_shape=(jax...  52.3 us
    unnamed x10, local copies, waits for them, and re-layouts  4.06 us

profile of v1, /device:TPU:0, one launch (start us, length us, event | category | flops | bytes accessed | tf_op | source)
XLA Modules:
  0.0 57.1 jit_solution(7597777680999720415)
XLA Ops:
  0.6 0.0 copy-start
  0.6 0.0 copy-start.1
  0.7 0.0 copy-start.2
  0.7 1.4 %copy.11 = bf16[8,8,48,128]{3,1,2,0:T(8,128)(2,1)S(1)} copy(bf16[8,8,48,128]{3,2,1,0:T(8,128)(2,1)} %bitcast.18) | data formatting | bytes 1572864
  2.0 0.0 copy-done
  2.1 0.0 copy-done.1
  2.1 0.0 copy-done.2
  2.1 52.3 %step.1 = (f32[1,6144]{1,0:T(1,128)S(1)}, f32[64,6144]{1,0:T(8,128)S(1)}, f32[64,384]{1,0:T(8,128)S(1)}) custom-call(f32[1,6144]{1,0:T(1,128)S(1)} %bitcast.16, bf16[64,6144]{1,0:T(8,128)(2,1)S(1)} %bitcast.13, bf16[64,384]{1,0:T(8,128)(2,1)S(1)} %copy-done.1, f32[64,384]{1,0:T(8,128)S(1)} %copy-done), custom_call_target="tpu_custom_call" | custom-call | tf_op jit(solution)/shard_map/step/pallas_call | solution.py:333
  54.4 1.4 %copy.9 = f32[8,8,48,128]{3,2,1,0:T(8,128)} copy(f32[8,8,48,128]{3,1,2,0:T(8,128)S(1)} %bitcast.14) | data formatting | bytes 3145728
  55.8 0.6 %copy.14 = f32[1,48,128]{2,1,0:T(8,128)} copy(f32[1,48,128]{2,1,0:T(8,128)S(1)} %bitcast.15) | data formatting | bytes 49152
  56.5 0.6 %copy.15 = f32[64,384]{1,0:T(8,128)} copy(f32[64,384]{1,0:T(8,128)S(1)} %get-tuple-element.17) | data formatting | bytes 196608
Async XLA Ops:
  0.6 1.4 %copy-start = (f32[64,384]{1,0:T(8,128)S(1)}, f32[64,384]{1,0:T(8,128)}, u32[]{:S(2)}) copy-start(f32[64,384]{1,0:T(8,128)} %kicks_ref.1) | copy-start | bytes 294916
  0.6 1.4 %copy-start.1 = (bf16[64,384]{1,0:T(8,128)(2,1)S(1)}, bf16[64,384]{1,0:T(8,128)(2,1)}, u32[]{:S(2)}) copy-start(bf16[64,384]{1,0:T(8,128)(2,1)} %coeffs_ref.1) | copy-start | bytes 147460
  0.7 1.4 %copy-start.2 = (f32[1,48,128]{2,1,0:T(8,128)S(1)}, f32[1,48,128]{2,1,0:T(8,128)}, u32[]{:S(2)}) copy-start(f32[1,48,128]{2,1,0:T(8,128)} %param.4) | copy-start | bytes 73732
